TPU v7x, 32 devices: a whole 2x2x4 slice. The times are simulated.
32 devices in a mesh: sec: 8 (over z, x), fld: 4 (over y, core).
Axes of the slice: x: 2, y: 2, z: 4, core: 2. Of those that a mesh axis runs over, the one named last changes fastest.
Arguments:
- surface: float32 [4, 256, 512], P('fld', 'sec'), may hold values from -6 to 6
- diffusivity: float32 [4, 256, 512], P('fld', 'sec'), may hold values from 0.02 to 0.24
- send_list: int32 [8, 8, 171], P('sec'), may hold values from 0 to 127
- recv_slot: int32 [1024, 4], P('sec'), may hold values from 0 to 1367, as said below
- weights: bfloat16 [1024, 4, 128, 128], P(('sec', 'fld')), may hold values from -0.25 to 0.25
Outputs:
- stepped: float32 [4, 256, 512], P('fld', 'sec')
- remapped: float32 [4, 256, 512], P('fld', 'sec')
Inputs may be any that keep to these rules, and one draw needn't show every extreme that they name: `recv_slot`: the 512 entries of one device's target blocks are distinct slots, all of devices of the other component; from one source device to one target device at most 171 slots are used, and that many in some pair.
All inputs are finite; a program needn't handle non-finite values.
Results may differ from a plain program's by a relative error of at most 0.0029.
Values may be sent and summed in bfloat16 or wider, within the bound.
A program may use at most 64 MiB of HBM per device.

v0:
```python
import jax
import jax.numpy as jnp
from jax import lax
from jax.sharding import PartitionSpec as P

SUBSTEPS = 4


def padded(block, sides, width):
    for axis, dim in sides:
        count = lax.axis_size(axis)
        forward = [(i, i + 1) for i in range(count - 1)]
        backward = [(target, source) for source, target in forward]
        low = lax.ppermute(
            lax.slice_in_dim(block, block.shape[dim] - width, None, axis=dim), axis, forward
        )
        high = lax.ppermute(lax.slice_in_dim(block, 0, width, axis=dim), axis, backward)
        block = jnp.concatenate([low, block, high], axis=dim)
    return block


def valid_rows(count, first, lowest, highest):
    global_row = first + jnp.arange(count, dtype=jnp.int32)
    return ((global_row >= lowest) & (global_row < highest))[None, :, None]


def update(extended, kappa):
    upper = extended[:, :-2]
    lower = extended[:, 2:]
    middle = extended[:, 1:-1]
    lap = upper + lower + jnp.roll(middle, 1, 2) + jnp.roll(middle, -1, 2) - 4.0 * middle
    return middle + kappa * lap


def per_device(surface, diffusivity, send_list, recv_slot, weights):
    sec_count = lax.axis_size("sec")
    here = lax.axis_index("sec")
    rows = surface.shape[1]
    cols = surface.shape[2]
    atmos_count = sec_count * 3 // 8
    is_ocean = here >= atmos_count
    lowest = jnp.where(is_ocean, atmos_count * rows, 0)
    highest = jnp.where(is_ocean, sec_count * rows, atmos_count * rows)
    field = surface
    for step in range(SUBSTEPS):
        extended = padded(field, (("sec", 1),), 1)
        inside = valid_rows(rows + 2, here * rows - 1, lowest, highest)
        extended = jnp.where(inside, extended, 0.0)
        field = update(extended, diffusivity)
    blocks = field.reshape(-1, 128).astype(jnp.bfloat16)
    outgoing = blocks[send_list[0]]
    incoming = lax.all_to_all(outgoing, "sec", split_axis=0, concat_axis=0, tiled=True)
    flat = incoming.reshape(-1, 128)
    pairs = flat[recv_slot]
    gathered = lax.all_to_all(pairs[None], "fld", split_axis=1, concat_axis=0, tiled=True)
    result = jnp.einsum("tkij,ftkj->fti", weights, gathered, preferred_element_type=jnp.float32)
    returned = lax.all_to_all(result, "fld", split_axis=0, concat_axis=1, tiled=True)
    remapped = returned.reshape(1, rows, cols)
    return (field, remapped)


def solution(mesh):
    return jax.shard_map(
        per_device,
        mesh=mesh,
        in_specs=(
            P("fld", "sec", None),
            P("fld", "sec", None),
            P("sec", None, None),
            P("sec", None),
            P(("sec", "fld"), None, None, None),
        ),
        out_specs=(P("fld", "sec", None), P("fld", "sec", None)),
        check_vma=False,
    )
```

profile of v0, /device:TPU:0, one launch (start us, length us, event | category | flops | bytes accessed | tf_op | source)
XLA Modules:
  0.0 82.4 jit_solution(17160284931847837862)
XLA Ops:
  0.6 0.7 fusion.34
  1.4 1.3 %collective-permute-start.1 = (f32[1,1,512]{2,1,0:T(1,128)S(1)}, f32[1,1,512]{2,1,0:T(1,128)S(1)}, u32[]{:S(2)}, u32[]{:S(2)}) collective-permute-start(f32[1,1,512]{2,1,0:T(1,128)S(1)} %get-tuple-element.27), channel_id=1, source_target_pairs={{4,0},{8,4},{12,8},{16,12},{20,16},{24,20},{28,24},{5,1},{9,5},{13... | collective-permute-start | bytes 6152 | tf_op jit(solution)/shard_map/ppermute | solution.py:17
  2.7 5.5 %collective-permute-start = (f32[1,1,512]{2,1,0:T(1,128)S(1)}, f32[1,1,512]{2,1,0:T(1,128)S(1)}, u32[]{:S(2)}, u32[]{:S(2)}) collective-permute-start(f32[1,1,512]{2,1,0:T(1,128)S(1)} %get-tuple-element.26), channel_id=1, source_target_pairs={{0,4},{4,8},{8,12},{12,16},{16,20},{20,24},{24,28},{1,5},{5,9},{9,... | collective-permute-start | bytes 6152 | tf_op jit(solution)/shard_map/ppermute | solution.py:14
  8.2 0.0 collective-permute-done.1
  8.2 1.3 %collective-permute-done = f32[1,1,512]{2,1,0:T(1,128)S(1)} collective-permute-done((f32[1,1,512]{2,1,0:T(1,128)S(1)}, f32[1,1,512]{2,1,0:T(1,128)S(1)}, u32[]{:S(2)}, u32[]{:S(2)}) %collective-permute-start) | collective-permute-done | bytes 2080 | tf_op jit(solution)/shard_map/ppermute | solution.py:14
  9.4 0.9 %maximum_select_fusion = f32[1,34,512]{2,1,0:T(8,128)S(1)} fusion(f32[1,1,512]{2,1,0:T(1,128)S(1)} %collective-permute-done.1, f32[1,32,512]{2,1,0:T(8,128)} %param.5, f32[1,1,512]{2,1,0:T(1,128)S(1)} %collective-permute-done, pred[34]{0:T(512)(128)(4,1)S(1)} %compare_and_fusion), kind=kLoop, calls=%fused_computation.4 | loop fusion | flops 52224 | bytes 139298 | tf_op jit(solution)/shard_map/jit(_where)/select_n | solution.py:48
  10.3 0.1 fusion.29
  10.4 0.0 copy-start
  10.4 0.1 fusion.30
  10.5 0.9 %fusion.20 = f32[1,32,512]{2,1,0:T(8,128)S(1)} fusion(f32[1,32,512]{2,1,0:T(8,128)} %param.6, f32[1,34,512]{2,1,0:T(8,128)S(1)} %maximum_select_fusion, f32[1,32,511]{2,1,0:T(8,128)S(1)} %get-tuple-element.17, f32[1,32,1]{2,1,0:T(8,128)S(1)} %get-tuple-element.19, f32[1,32,1]{2,1,0:T(8,128)S(1)} %get-tuple-element.18, f32[1,32,511]{2,1,0:T(8,128)S(1)} %get-tuple-element.16), kind=kLoop, calls=%fused_computation.31 | loop fusion | flops 147456 | bytes 458752 | tf_op jit(solution)/shard_map/add | solution.py:32
  11.5 1.3 %collective-permute-start.3 = (f32[1,1,512]{2,1,0:T(1,128)S(1)}, f32[1,1,512]{2,1,0:T(1,128)S(1)}, u32[]{:S(2)}, u32[]{:S(2)}) collective-permute-start(f32[1,1,512]{2,1,0:T(1,128)S(1)} %get-tuple-element.25), channel_id=1, source_target_pairs={{4,0},{8,4},{12,8},{16,12},{20,16},{24,20},{28,24},{5,1},{9,5},{13... | collective-permute-start | bytes 6152 | tf_op jit(solution)/shard_map/ppermute | solution.py:17
  12.8 5.4 %collective-permute-start.2 = (f32[1,1,512]{2,1,0:T(1,128)S(1)}, f32[1,1,512]{2,1,0:T(1,128)S(1)}, u32[]{:S(2)}, u32[]{:S(2)}) collective-permute-start(f32[1,1,512]{2,1,0:T(1,128)S(1)} %get-tuple-element.24), channel_id=1, source_target_pairs={{0,4},{4,8},{8,12},{12,16},{16,20},{20,24},{24,28},{1,5},{5,9},{9,... | collective-permute-start | bytes 6152 | tf_op jit(solution)/shard_map/ppermute | solution.py:14
  18.2 0.0 collective-permute-done.3
  18.2 1.3 %collective-permute-done.2 = f32[1,1,512]{2,1,0:T(1,128)S(1)} collective-permute-done((f32[1,1,512]{2,1,0:T(1,128)S(1)}, f32[1,1,512]{2,1,0:T(1,128)S(1)}, u32[]{:S(2)}, u32[]{:S(2)}) %collective-permute-start.2) | collective-permute-done | bytes 2080 | tf_op jit(solution)/shard_map/ppermute | solution.py:14
  19.5 0.1 maximum_select_fusion.1
  19.6 0.1 fusion.27
  19.7 0.1 fusion.28
  19.8 0.9 %fusion.15 = f32[1,32,512]{2,1,0:T(8,128)S(1)} fusion(f32[1,32,512]{2,1,0:T(8,128)} %param.6, f32[1,34,512]{2,1,0:T(8,128)S(1)} %maximum_select_fusion.1, f32[1,32,511]{2,1,0:T(8,128)S(1)} %get-tuple-element.13, f32[1,32,1]{2,1,0:T(8,128)S(1)} %get-tuple-element.15, f32[1,32,1]{2,1,0:T(8,128)S(1)} %get-tuple-element.14, f32[1,32,511]{2,1,0:T(8,128)S(1)} %get-tuple-element.12), kind=kLoop, calls=%fused_computation.25 | loop fusion | flops 147456 | bytes 458752 | tf_op jit(solution)/shard_map/add | solution.py:32
  20.7 1.3 %collective-permute-start.5 = (f32[1,1,512]{2,1,0:T(1,128)S(1)}, f32[1,1,512]{2,1,0:T(1,128)S(1)}, u32[]{:S(2)}, u32[]{:S(2)}) collective-permute-start(f32[1,1,512]{2,1,0:T(1,128)S(1)} %get-tuple-element.23), channel_id=1, source_target_pairs={{4,0},{8,4},{12,8},{16,12},{20,16},{24,20},{28,24},{5,1},{9,5},{13... | collective-permute-start | bytes 6152 | tf_op jit(solution)/shard_map/ppermute | solution.py:17
  22.0 5.7 %collective-permute-start.4 = (f32[1,1,512]{2,1,0:T(1,128)S(1)}, f32[1,1,512]{2,1,0:T(1,128)S(1)}, u32[]{:S(2)}, u32[]{:S(2)}) collective-permute-start(f32[1,1,512]{2,1,0:T(1,128)S(1)} %get-tuple-element.22), channel_id=1, source_target_pairs={{0,4},{4,8},{8,12},{12,16},{16,20},{20,24},{24,28},{1,5},{5,9},{9,... | collective-permute-start | bytes 6152 | tf_op jit(solution)/shard_map/ppermute | solution.py:14
  27.7 0.7 compare_select_fusion
  28.4 0.1 reshape.296
  28.5 0.0 collective-permute-done.5
  28.5 0.5 collective-permute-done.4
  29.0 0.1 maximum_select_fusion.2
  29.1 0.1 fusion.25
  29.2 0.1 fusion.26
  29.3 0.9 %fusion.10 = f32[1,32,512]{2,1,0:T(8,128)S(1)} fusion(f32[1,32,512]{2,1,0:T(8,128)} %param.6, f32[1,34,512]{2,1,0:T(8,128)S(1)} %maximum_select_fusion.2, f32[1,32,511]{2,1,0:T(8,128)S(1)} %get-tuple-element.9, f32[1,32,1]{2,1,0:T(8,128)S(1)} %get-tuple-element.11, f32[1,32,1]{2,1,0:T(8,128)S(1)} %get-tuple-element.10, f32[1,32,511]{2,1,0:T(8,128)S(1)} %get-tuple-element.8), kind=kLoop, calls=%fused_computation.19 | loop fusion | flops 147456 | bytes 458752 | tf_op jit(solution)/shard_map/add | solution.py:32
  30.2 1.3 %collective-permute-start.7 = (f32[1,1,512]{2,1,0:T(1,128)S(1)}, f32[1,1,512]{2,1,0:T(1,128)S(1)}, u32[]{:S(2)}, u32[]{:S(2)}) collective-permute-start(f32[1,1,512]{2,1,0:T(1,128)S(1)} %get-tuple-element.21), channel_id=1, source_target_pairs={{4,0},{8,4},{12,8},{16,12},{20,16},{24,20},{28,24},{5,1},{9,5},{13... | collective-permute-start | bytes 6152 | tf_op jit(solution)/shard_map/ppermute | solution.py:17
  31.5 5.7 %collective-permute-start.6 = (f32[1,1,512]{2,1,0:T(1,128)S(1)}, f32[1,1,512]{2,1,0:T(1,128)S(1)}, u32[]{:S(2)}, u32[]{:S(2)}) collective-permute-start(f32[1,1,512]{2,1,0:T(1,128)S(1)} %get-tuple-element.20), channel_id=1, source_target_pairs={{0,4},{4,8},{8,12},{12,16},{16,20},{20,24},{24,28},{1,5},{5,9},{9,... | collective-permute-start | bytes 6152 | tf_op jit(solution)/shard_map/ppermute | solution.py:14
  37.2 0.0 collective-permute-done.7
  37.3 1.3 %collective-permute-done.6 = f32[1,1,512]{2,1,0:T(1,128)S(1)} collective-permute-done((f32[1,1,512]{2,1,0:T(1,128)S(1)}, f32[1,1,512]{2,1,0:T(1,128)S(1)}, u32[]{:S(2)}, u32[]{:S(2)}) %collective-permute-start.6) | collective-permute-done | bytes 2080 | tf_op jit(solution)/shard_map/ppermute | solution.py:14
  38.5 0.1 maximum_select_fusion.3
  38.6 0.1 fusion.23
  38.7 0.1 fusion.24
  38.8 1.6 %fusion.21 = (bf16[1,32,512]{2,1,0:T(8,128)(2,1)S(1)}, f32[1,32,512]{2,1,0:T(8,128)}) fusion(f32[1,32,512]{2,1,0:T(8,128)} %param.6, f32[1,32,1]{2,1,0:T(8,128)S(1)} %get-tuple-element.5, f32[1,32,511]{2,1,0:T(8,128)S(1)} %get-tuple-element.7, f32[1,32,511]{2,1,0:T(8,128)S(1)} %get-tuple-element.6, f32[1,32,1]{2,1,0:T(8,128)S(1)} %get-tuple-element.4, ...), kind=kLoop, calls=%fused_computation.37 | loop fusion | flops 163840 | bytes 491520 | tf_op jit(solution)/shard_map/convert_element_type | solution.py:50
  40.4 3.3 %gather_fusion = bf16[1368,128]{1,0:T(8,128)(2,1)S(1)} fusion(bf16[128,128]{1,0:T(8,128)(2,1)S(1)} %convert_element_type.7, s32[2048]{0:T(1024)S(1)} %pad_clamp_fusion), kind=kCustom, calls=%fused_computation | custom fusion | bytes 705888 | tf_op jit(solution)/shard_map/gather | solution.py:51
  43.7 0.8 %reshape.295 = bf16[8,171,128]{2,1,0:T(8,128)(2,1)} reshape(bf16[1368,128]{1,0:T(8,128)(2,1)S(1)} %gather_fusion) | data formatting | bytes 700416 | tf_op jit(solution)/shard_map/gather | solution.py:51
  44.5 9.7 %all-to-all-start = ((bf16[8,171,128]{2,1,0:T(8,128)(2,1)}), bf16[8,171,128]{2,1,0:T(8,128)(2,1)S(1)}, u32[]{:S(2)}, u32[]{:S(2)}) async-start(bf16[8,171,128]{2,1,0:T(8,128)(2,1)} %reshape.295), calls=%async_computation | async-start | bytes 720896 | tf_op jit(solution)/shard_map/all_to_all | solution.py:52
  54.3 0.0 copy-done
  54.3 0.1 copy.11
  54.4 0.1 reshape.304
  54.5 8.7 %all-to-all-done = bf16[8,171,128]{2,1,0:T(8,128)(2,1)S(1)} async-done(((bf16[8,171,128]{2,1,0:T(8,128)(2,1)}), bf16[8,171,128]{2,1,0:T(8,128)(2,1)S(1)}, u32[]{:S(2)}, u32[]{:S(2)}) %all-to-all-start) | async-done | bytes 350240 | tf_op jit(solution)/shard_map/all_to_all | solution.py:52
  63.2 0.1 reshape.292
  63.3 1.3 %gather_fusion.1 = bf16[512,128]{1,0:T(8,128)(2,1)S(1)} fusion(bf16[1368,128]{1,0:T(8,128)(2,1)S(1)} %reshape.292, s32[1024]{0:T(1024)S(1)} %pad_clamp_fusion.1), kind=kCustom, calls=%fused_computation.1 | custom fusion | bytes 264192 | tf_op jit(solution)/shard_map/gather | solution.py:54
  64.7 7.2 %all_to_all.26 = bf16[1,128,4,128]{3,2,0,1:T(4,128)(2,1)S(1)} all-to-all(bf16[1,128,4,128]{3,2,0,1:T(4,128)(2,1)S(1)} %bitcast.14), channel_id=1, replica_groups=mesh['sec'=8,'fld'=4] {'fld'}, dimensions={1} | all-to-all | bytes 262144 | tf_op jit(solution)/shard_map/all_to_all | solution.py:55
  71.9 3.4 %convolution_bitcast_fusion = f32[4,32,128]{2,0,1:T(4,128)S(1)} fusion(bf16[32,4,128,128]{3,2,1,0:T(8,128)(2,1)} %param.9, bf16[4,32,4,128]{3,2,1,0:T(4,128)(2,1)S(1)} %bitcast.15), kind=kOutput, calls=%fused_computation.2 | convolution fusion | flops 16777216 | bytes 4390912 | tf_op jit(solution)/shard_map/tkij,ftkj->fti/dot_general | solution.py:56
  75.3 6.5 %all_to_all.27 = f32[4,32,128]{2,1,0:T(8,128)S(1)} all-to-all(f32[4,32,128]{2,1,0:T(8,128)S(1)} %copy.15), channel_id=1, replica_groups=mesh['sec'=8,'fld'=4] {'fld'}, dimensions={0} | all-to-all | bytes 131072 | tf_op jit(solution)/shard_map/all_to_all | solution.py:57
  81.8 0.6 reshape.293
  (9 shorter events, 0.1 us)
Async XLA Ops:
  1.4 6.8 %collective-permute-start.1 = (f32[1,1,512]{2,1,0:T(1,128)S(1)}, f32[1,1,512]{2,1,0:T(1,128)S(1)}, u32[]{:S(2)}, u32[]{:S(2)}) collective-permute-start(f32[1,1,512]{2,1,0:T(1,128)S(1)} %get-tuple-element.27), channel_id=1, source_target_pairs={{4,0},{8,4},{12,8},{16,12},{20,16},{24,20},{28,24},{5,1},{9,5},{13... | collective-permute-start | bytes 6152 | tf_op jit(solution)/shard_map/ppermute | solution.py:17
  2.7 6.8 %collective-permute-start = (f32[1,1,512]{2,1,0:T(1,128)S(1)}, f32[1,1,512]{2,1,0:T(1,128)S(1)}, u32[]{:S(2)}, u32[]{:S(2)}) collective-permute-start(f32[1,1,512]{2,1,0:T(1,128)S(1)} %get-tuple-element.26), channel_id=1, source_target_pairs={{0,4},{4,8},{8,12},{12,16},{16,20},{20,24},{24,28},{1,5},{5,9},{9,... | collective-permute-start | bytes 6152 | tf_op jit(solution)/shard_map/ppermute | solution.py:14
  10.4 43.8 %copy-start = (s32[128,4]{0,1:T(4,128)S(1)}, s32[128,4]{0,1:T(4,128)}, u32[]{:S(2)}) copy-start(s32[128,4]{0,1:T(4,128)} %param.8) | copy-start | bytes 6148
  11.5 6.8 %collective-permute-start.3 = (f32[1,1,512]{2,1,0:T(1,128)S(1)}, f32[1,1,512]{2,1,0:T(1,128)S(1)}, u32[]{:S(2)}, u32[]{:S(2)}) collective-permute-start(f32[1,1,512]{2,1,0:T(1,128)S(1)} %get-tuple-element.25), channel_id=1, source_target_pairs={{4,0},{8,4},{12,8},{16,12},{20,16},{24,20},{28,24},{5,1},{9,5},{13... | collective-permute-start | bytes 6152 | tf_op jit(solution)/shard_map/ppermute | solution.py:17
  12.8 6.7 %collective-permute-start.2 = (f32[1,1,512]{2,1,0:T(1,128)S(1)}, f32[1,1,512]{2,1,0:T(1,128)S(1)}, u32[]{:S(2)}, u32[]{:S(2)}) collective-permute-start(f32[1,1,512]{2,1,0:T(1,128)S(1)} %get-tuple-element.24), channel_id=1, source_target_pairs={{0,4},{4,8},{8,12},{12,16},{16,20},{20,24},{24,28},{1,5},{5,9},{9,... | collective-permute-start | bytes 6152 | tf_op jit(solution)/shard_map/ppermute | solution.py:14
  20.7 7.8 %collective-permute-start.5 = (f32[1,1,512]{2,1,0:T(1,128)S(1)}, f32[1,1,512]{2,1,0:T(1,128)S(1)}, u32[]{:S(2)}, u32[]{:S(2)}) collective-permute-start(f32[1,1,512]{2,1,0:T(1,128)S(1)} %get-tuple-element.23), channel_id=1, source_target_pairs={{4,0},{8,4},{12,8},{16,12},{20,16},{24,20},{28,24},{5,1},{9,5},{13... | collective-permute-start | bytes 6152 | tf_op jit(solution)/shard_map/ppermute | solution.py:17
  22.0 7.0 %collective-permute-start.4 = (f32[1,1,512]{2,1,0:T(1,128)S(1)}, f32[1,1,512]{2,1,0:T(1,128)S(1)}, u32[]{:S(2)}, u32[]{:S(2)}) collective-permute-start(f32[1,1,512]{2,1,0:T(1,128)S(1)} %get-tuple-element.22), channel_id=1, source_target_pairs={{0,4},{4,8},{8,12},{12,16},{16,20},{20,24},{24,28},{1,5},{5,9},{9,... | collective-permute-start | bytes 6152 | tf_op jit(solution)/shard_map/ppermute | solution.py:14
  30.2 7.0 %collective-permute-start.7 = (f32[1,1,512]{2,1,0:T(1,128)S(1)}, f32[1,1,512]{2,1,0:T(1,128)S(1)}, u32[]{:S(2)}, u32[]{:S(2)}) collective-permute-start(f32[1,1,512]{2,1,0:T(1,128)S(1)} %get-tuple-element.21), channel_id=1, source_target_pairs={{4,0},{8,4},{12,8},{16,12},{20,16},{24,20},{28,24},{5,1},{9,5},{13... | collective-permute-start | bytes 6152 | tf_op jit(solution)/shard_map/ppermute | solution.py:17
  31.5 7.0 %collective-permute-start.6 = (f32[1,1,512]{2,1,0:T(1,128)S(1)}, f32[1,1,512]{2,1,0:T(1,128)S(1)}, u32[]{:S(2)}, u32[]{:S(2)}) collective-permute-start(f32[1,1,512]{2,1,0:T(1,128)S(1)} %get-tuple-element.20), channel_id=1, source_target_pairs={{0,4},{4,8},{8,12},{12,16},{16,20},{20,24},{24,28},{1,5},{5,9},{9,... | collective-permute-start | bytes 6152 | tf_op jit(solution)/shard_map/ppermute | solution.py:14
  44.5 18.7 %all-to-all-start = ((bf16[8,171,128]{2,1,0:T(8,128)(2,1)}), bf16[8,171,128]{2,1,0:T(8,128)(2,1)S(1)}, u32[]{:S(2)}, u32[]{:S(2)}) async-start(bf16[8,171,128]{2,1,0:T(8,128)(2,1)} %reshape.295), calls=%async_computation | async-start | bytes 720896 | tf_op jit(solution)/shard_map/all_to_all | solution.py:52
where the time goes:
time: 83.2 us; the launch traced here: 82.4 us
  starting transfers between devices  37.2 us (45%)
  blocking collectives  13.7 us (16%)
  waiting for transfers between devices  13 us (16%)
  local copies, waits for them, and re-layouts  8 us (10%)
  other arithmetic  6.24 us (8%)
  matrix products  3.38 us (4%)
  between operations  0.88 us (1%)
    ppermute x4, starting transfers between devices, padded(): lax.ppermute(lax.slice_in_dim(block, block.shape[dim] - width, None, axis...  22.3 us
    all_to_all x1, starting transfers between devices, per_device(): lax.all_to_all(outgoing, 'sec', split_axis=0, concat_axis=0, tiled=True)  9.72 us
    all_to_all x1, waiting for transfers between devices, per_device(): lax.all_to_all(outgoing, 'sec', split_axis=0, concat_axis=0, tiled=True)  8.69 us
    all_to_all x1, blocking collectives, per_device(): lax.all_to_all(pairs[None], 'fld', split_axis=1, concat_axis=0, tiled=True)  7.22 us
    all_to_all x1, blocking collectives, per_device(): lax.all_to_all(result, 'fld', split_axis=0, concat_axis=1, tiled=True)  6.49 us
    ppermute x4, starting transfers between devices, padded(): lax.ppermute(lax.slice_in_dim(block, 0, width, axis=dim), axis, backward)  5.16 us
    ppermute x4, waiting for transfers between devices, padded(): lax.ppermute(lax.slice_in_dim(block, block.shape[dim] - width, None, axis...  4.29 us
    gather x2, local copies, waits for them, and re-layouts, per_device(): outgoing = blocks[send_list[0]]  4.17 us
  transfers between devices with their start and end apart: 9, of which 5 were waited for; matrix products, arithmetic and copies ran while one was open for 1% of the time, Pallas kernels for 0%

commit v1 on v0

--- a/solution.py
+++ b/solution.py
@@ -54,7 +54,21 @@
     pairs = flat[recv_slot]
     gathered = lax.all_to_all(pairs[None], "fld", split_axis=1, concat_axis=0, tiled=True)
     result = jnp.einsum("tkij,ftkj->fti", weights, gathered, preferred_element_type=jnp.float32)
-    returned = lax.all_to_all(result, "fld", split_axis=0, concat_axis=1, tiled=True)
+    s_next = lax.axis_size("fld")
+    y_new = lax.axis_index("fld")
+    ready, state_now = (s_next, y_new)
+    small = result.shape[0] // ready
+    a_next = jnp.roll(result, -state_now * small, 0)
+    formed = lax.slice_in_dim(a_next, 0, small, axis=0)
+    all_blocks = [formed]
+    for jj in range(1, ready):
+        met_up = lax.slice_in_dim(a_next, jj * small, (jj + 1) * small, axis=0)
+        block_last = lax.ppermute(
+            met_up, "fld", [(hop_no, (hop_no + jj) % ready) for hop_no in range(ready)]
+        )
+        all_blocks.append(block_last)
+    r1 = jnp.concatenate(all_blocks[::-1], 1)
+    returned = jnp.roll(r1, (state_now + 1) * all_blocks[0].shape[1], 1)
     remapped = returned.reshape(1, rows, cols)
     return (field, remapped)
 

time: 83.2 us -> 83 us (level)
  waiting for transfers between devices: 13 us -> 32.3 us
  blocking collectives: 13.7 us -> 0 us
  starting transfers between devices: 37.2 us -> 30.3 us
  local copies, waits for them, and re-layouts: 8 us -> 8.87 us
    ppermute x4, waiting for transfers between devices: 0.01 us -> 15.8 us  [padded(): lax.ppermute(lax.slice_in_dim(block, 0, width, axis=dim), axis, backward)]
    all_to_all x2 -> x0, blocking collectives: 13.7 us -> none  [the longest x1 7.22 us: per_device(): lax.all_to_all(pairs[None], 'fld', split_axis=1, concat_axis=0, tiled=True)]
    all_to_all x1, starting transfers between devices: 9.72 us -> 3.78 us  [per_device(): lax.all_to_all(outgoing, 'sec', split_axis=0, concat_axis=0, tiled=True)]
    ppermute x4, starting transfers between devices: 22.3 us -> 16.9 us  [padded(): lax.ppermute(lax.slice_in_dim(block, block.shape[dim] - width, None, axis...]
    all_to_all x0 -> x1, waiting for transfers between devices: none -> 4.57 us  [per_device(): lax.all_to_all(pairs[None], 'fld', split_axis=1, concat_axis=0, tiled=True)]
    ppermute x4, waiting for transfers between devices: 4.29 us -> 0.01 us  [padded(): lax.ppermute(lax.slice_in_dim(block, block.shape[dim] - width, None, axis...]
    all_to_all x0 -> x1, starting transfers between devices: none -> 3.32 us  [per_device(): lax.all_to_all(pairs[None], 'fld', split_axis=1, concat_axis=0, tiled=True)]
    ppermute x0 -> x3, waiting for transfers between devices: none -> 3.15 us  [per_device(): lax.ppermute(met_up, 'fld', [(hop_no, (hop_no + jj) % ready) for hop_no i...]
  transfers between devices with their start and end apart: 9 -> 13, of which waited for: 5 -> 9; matrix products, arithmetic and copies ran while one was open for 1% -> 1% of each run, Pallas kernels for 0% -> 0%
where the time goes in v1:
time: 83 us; the launch traced here: 82.1 us
  waiting for transfers between devices  32.3 us (39%)
  starting transfers between devices  30.3 us (37%)
  local copies, waits for them, and re-layouts  8.87 us (11%)
  other arithmetic  6.31 us (8%)
  matrix products  3.37 us (4%)
  between operations  0.97 us (1%)
    ppermute x4, starting transfers between devices, padded(): lax.ppermute(lax.slice_in_dim(block, block.shape[dim] - width, None, axis...  16.9 us
    ppermute x4, waiting for transfers between devices, padded(): lax.ppermute(lax.slice_in_dim(block, 0, width, axis=dim), axis, backward)  15.8 us
    all_to_all x1, waiting for transfers between devices, per_device(): lax.all_to_all(outgoing, 'sec', split_axis=0, concat_axis=0, tiled=True)  8.69 us
    ppermute x4, starting transfers between devices, padded(): lax.ppermute(lax.slice_in_dim(block, 0, width, axis=dim), axis, backward)  5.17 us
    all_to_all x1, waiting for transfers between devices, per_device(): lax.all_to_all(pairs[None], 'fld', split_axis=1, concat_axis=0, tiled=True)  4.57 us
    gather x2, local copies, waits for them, and re-layouts, per_device(): outgoing = blocks[send_list[0]]  4.16 us
    all_to_all x1, starting transfers between devices, per_device(): lax.all_to_all(outgoing, 'sec', split_axis=0, concat_axis=0, tiled=True)  3.78 us
    dot_general x1, matrix products, per_device(): jnp.einsum('tkij,ftkj->fti', weights, gathered, preferred_element_type=jn...  3.37 us
  transfers between devices with their start and end apart: 13, of which 9 were waited for; matrix products, arithmetic and copies ran while one was open for 1% of the time, Pallas kernels for 0%

profile of v1, /device:TPU:0, one launch (start us, length us, event | category | flops | bytes accessed | tf_op | source)
XLA Modules:
  0.0 82.1 jit_solution(6985509997546181005)
XLA Ops:
  0.6 0.7 fusion.36
  1.4 4.8 %collective-permute-start = (f32[1,1,512]{2,1,0:T(1,128)S(1)}, f32[1,1,512]{2,1,0:T(1,128)S(1)}, u32[]{:S(2)}, u32[]{:S(2)}) collective-permute-start(f32[1,1,512]{2,1,0:T(1,128)S(1)} %get-tuple-element.29), channel_id=1, source_target_pairs={{0,4},{4,8},{8,12},{12,16},{16,20},{20,24},{24,28},{1,5},{5,9},{9,... | collective-permute-start | bytes 6152 | tf_op jit(solution)/shard_map/ppermute | solution.py:14
  6.2 1.3 %collective-permute-start.1 = (f32[1,1,512]{2,1,0:T(1,128)S(1)}, f32[1,1,512]{2,1,0:T(1,128)S(1)}, u32[]{:S(2)}, u32[]{:S(2)}) collective-permute-start(f32[1,1,512]{2,1,0:T(1,128)S(1)} %get-tuple-element.30), channel_id=1, source_target_pairs={{4,0},{8,4},{12,8},{16,12},{20,16},{24,20},{28,24},{5,1},{9,5},{13... | collective-permute-start | bytes 6152 | tf_op jit(solution)/shard_map/ppermute | solution.py:17
  7.5 0.0 collective-permute-done
  7.5 4.1 %collective-permute-done.1 = f32[1,1,512]{2,1,0:T(1,128)S(1)} collective-permute-done((f32[1,1,512]{2,1,0:T(1,128)S(1)}, f32[1,1,512]{2,1,0:T(1,128)S(1)}, u32[]{:S(2)}, u32[]{:S(2)}) %collective-permute-start.1) | collective-permute-done | bytes 2080 | tf_op jit(solution)/shard_map/ppermute | solution.py:17
  11.7 0.9 %maximum_select_fusion = f32[1,34,512]{2,1,0:T(8,128)S(1)} fusion(f32[1,1,512]{2,1,0:T(1,128)S(1)} %collective-permute-done.1, f32[1,32,512]{2,1,0:T(8,128)} %param.5, f32[1,1,512]{2,1,0:T(1,128)S(1)} %collective-permute-done, pred[34]{0:T(512)(128)(4,1)S(1)} %compare_and_fusion), kind=kLoop, calls=%fused_computation.6 | loop fusion | flops 52224 | bytes 139298 | tf_op jit(solution)/shard_map/jit(_where)/select_n | solution.py:48
  12.6 0.1 fusion.30
  12.7 0.0 copy-start
  12.7 0.1 fusion.31
  12.8 0.9 %fusion.21 = f32[1,32,512]{2,1,0:T(8,128)S(1)} fusion(f32[1,32,512]{2,1,0:T(8,128)} %param.6, f32[1,34,512]{2,1,0:T(8,128)S(1)} %maximum_select_fusion, f32[1,32,511]{2,1,0:T(8,128)S(1)} %get-tuple-element.17, f32[1,32,1]{2,1,0:T(8,128)S(1)} %get-tuple-element.19, f32[1,32,1]{2,1,0:T(8,128)S(1)} %get-tuple-element.18, f32[1,32,511]{2,1,0:T(8,128)S(1)} %get-tuple-element.16), kind=kLoop, calls=%fused_computation.34 | loop fusion | flops 147456 | bytes 458752 | tf_op jit(solution)/shard_map/add | solution.py:32
  13.7 4.4 %collective-permute-start.2 = (f32[1,1,512]{2,1,0:T(1,128)S(1)}, f32[1,1,512]{2,1,0:T(1,128)S(1)}, u32[]{:S(2)}, u32[]{:S(2)}) collective-permute-start(f32[1,1,512]{2,1,0:T(1,128)S(1)} %get-tuple-element.27), channel_id=1, source_target_pairs={{0,4},{4,8},{8,12},{12,16},{16,20},{20,24},{24,28},{1,5},{5,9},{9,... | collective-permute-start | bytes 6152 | tf_op jit(solution)/shard_map/ppermute | solution.py:14
  18.1 1.3 %collective-permute-start.3 = (f32[1,1,512]{2,1,0:T(1,128)S(1)}, f32[1,1,512]{2,1,0:T(1,128)S(1)}, u32[]{:S(2)}, u32[]{:S(2)}) collective-permute-start(f32[1,1,512]{2,1,0:T(1,128)S(1)} %get-tuple-element.28), channel_id=1, source_target_pairs={{4,0},{8,4},{12,8},{16,12},{20,16},{24,20},{28,24},{5,1},{9,5},{13... | collective-permute-start | bytes 6152 | tf_op jit(solution)/shard_map/ppermute | solution.py:17
  19.4 0.0 collective-permute-done.2
  19.4 4.2 %collective-permute-done.3 = f32[1,1,512]{2,1,0:T(1,128)S(1)} collective-permute-done((f32[1,1,512]{2,1,0:T(1,128)S(1)}, f32[1,1,512]{2,1,0:T(1,128)S(1)}, u32[]{:S(2)}, u32[]{:S(2)}) %collective-permute-start.3) | collective-permute-done | bytes 2080 | tf_op jit(solution)/shard_map/ppermute | solution.py:17
  23.6 0.1 maximum_select_fusion.1
  23.7 0.1 fusion.28
  23.7 0.1 fusion.29
  23.8 0.9 %fusion.16 = f32[1,32,512]{2,1,0:T(8,128)S(1)} fusion(f32[1,32,512]{2,1,0:T(8,128)} %param.6, f32[1,34,512]{2,1,0:T(8,128)S(1)} %maximum_select_fusion.1, f32[1,32,511]{2,1,0:T(8,128)S(1)} %get-tuple-element.13, f32[1,32,1]{2,1,0:T(8,128)S(1)} %get-tuple-element.15, f32[1,32,1]{2,1,0:T(8,128)S(1)} %get-tuple-element.14, f32[1,32,511]{2,1,0:T(8,128)S(1)} %get-tuple-element.12), kind=kLoop, calls=%fused_computation.28 | loop fusion | flops 147456 | bytes 458752 | tf_op jit(solution)/shard_map/add | solution.py:32
  24.8 3.4 %collective-permute-start.4 = (f32[1,1,512]{2,1,0:T(1,128)S(1)}, f32[1,1,512]{2,1,0:T(1,128)S(1)}, u32[]{:S(2)}, u32[]{:S(2)}) collective-permute-start(f32[1,1,512]{2,1,0:T(1,128)S(1)} %get-tuple-element.25), channel_id=1, source_target_pairs={{0,4},{4,8},{8,12},{12,16},{16,20},{20,24},{24,28},{1,5},{5,9},{9,... | collective-permute-start | bytes 6152 | tf_op jit(solution)/shard_map/ppermute | solution.py:14
  28.2 1.3 %collective-permute-start.5 = (f32[1,1,512]{2,1,0:T(1,128)S(1)}, f32[1,1,512]{2,1,0:T(1,128)S(1)}, u32[]{:S(2)}, u32[]{:S(2)}) collective-permute-start(f32[1,1,512]{2,1,0:T(1,128)S(1)} %get-tuple-element.26), channel_id=1, source_target_pairs={{4,0},{8,4},{12,8},{16,12},{20,16},{24,20},{28,24},{5,1},{9,5},{13... | collective-permute-start | bytes 6152 | tf_op jit(solution)/shard_map/ppermute | solution.py:17
  29.5 0.7 compare_select_fusion
  30.2 0.1 reshape.292
  30.3 0.0 collective-permute-done.4
  30.3 3.4 %collective-permute-done.5 = f32[1,1,512]{2,1,0:T(1,128)S(1)} collective-permute-done((f32[1,1,512]{2,1,0:T(1,128)S(1)}, f32[1,1,512]{2,1,0:T(1,128)S(1)}, u32[]{:S(2)}, u32[]{:S(2)}) %collective-permute-start.5) | collective-permute-done | bytes 2080 | tf_op jit(solution)/shard_map/ppermute | solution.py:17
  33.7 0.1 maximum_select_fusion.2
  33.7 0.1 fusion.26
  33.8 0.1 fusion.27
  33.9 0.9 %fusion.11 = f32[1,32,512]{2,1,0:T(8,128)S(1)} fusion(f32[1,32,512]{2,1,0:T(8,128)} %param.6, f32[1,34,512]{2,1,0:T(8,128)S(1)} %maximum_select_fusion.2, f32[1,32,511]{2,1,0:T(8,128)S(1)} %get-tuple-element.9, f32[1,32,1]{2,1,0:T(8,128)S(1)} %get-tuple-element.11, f32[1,32,1]{2,1,0:T(8,128)S(1)} %get-tuple-element.10, f32[1,32,511]{2,1,0:T(8,128)S(1)} %get-tuple-element.8), kind=kLoop, calls=%fused_computation.22 | loop fusion | flops 147456 | bytes 458752 | tf_op jit(solution)/shard_map/add | solution.py:32
  34.8 4.4 %collective-permute-start.6 = (f32[1,1,512]{2,1,0:T(1,128)S(1)}, f32[1,1,512]{2,1,0:T(1,128)S(1)}, u32[]{:S(2)}, u32[]{:S(2)}) collective-permute-start(f32[1,1,512]{2,1,0:T(1,128)S(1)} %get-tuple-element.23), channel_id=1, source_target_pairs={{0,4},{4,8},{8,12},{12,16},{16,20},{20,24},{24,28},{1,5},{5,9},{9,... | collective-permute-start | bytes 6152 | tf_op jit(solution)/shard_map/ppermute | solution.py:14
  39.2 1.3 %collective-permute-start.7 = (f32[1,1,512]{2,1,0:T(1,128)S(1)}, f32[1,1,512]{2,1,0:T(1,128)S(1)}, u32[]{:S(2)}, u32[]{:S(2)}) collective-permute-start(f32[1,1,512]{2,1,0:T(1,128)S(1)} %get-tuple-element.24), channel_id=1, source_target_pairs={{4,0},{8,4},{12,8},{16,12},{20,16},{24,20},{28,24},{5,1},{9,5},{13... | collective-permute-start | bytes 6152 | tf_op jit(solution)/shard_map/ppermute | solution.py:17
  40.5 0.0 collective-permute-done.6
  40.5 4.2 %collective-permute-done.7 = f32[1,1,512]{2,1,0:T(1,128)S(1)} collective-permute-done((f32[1,1,512]{2,1,0:T(1,128)S(1)}, f32[1,1,512]{2,1,0:T(1,128)S(1)}, u32[]{:S(2)}, u32[]{:S(2)}) %collective-permute-start.7) | collective-permute-done | bytes 2080 | tf_op jit(solution)/shard_map/ppermute | solution.py:17
  44.7 0.1 maximum_select_fusion.3
  44.8 0.1 fusion.25
  44.9 0.1 fusion.24
  44.9 1.6 %fusion.22 = (bf16[1,32,512]{2,1,0:T(8,128)(2,1)S(1)}, f32[1,32,512]{2,1,0:T(8,128)}) fusion(f32[1,32,512]{2,1,0:T(8,128)} %param.6, f32[1,32,1]{2,1,0:T(8,128)S(1)} %get-tuple-element.5, f32[1,32,511]{2,1,0:T(8,128)S(1)} %get-tuple-element.7, f32[1,32,511]{2,1,0:T(8,128)S(1)} %get-tuple-element.6, f32[1,32,1]{2,1,0:T(8,128)S(1)} %get-tuple-element.4, ...), kind=kLoop, calls=%fused_computation.49 | loop fusion | flops 163840 | bytes 491520 | tf_op jit(solution)/shard_map/convert_element_type | solution.py:50
  46.5 3.3 %gather_fusion = bf16[1368,128]{1,0:T(8,128)(2,1)S(1)} fusion(bf16[128,128]{1,0:T(8,128)(2,1)S(1)} %convert_element_type.7, s32[2048]{0:T(1024)S(1)} %pad_clamp_fusion), kind=kCustom, calls=%fused_computation | custom fusion | bytes 705888 | tf_op jit(solution)/shard_map/gather | solution.py:51
  49.9 0.8 %reshape.291 = bf16[8,171,128]{2,1,0:T(8,128)(2,1)} reshape(bf16[1368,128]{1,0:T(8,128)(2,1)S(1)} %gather_fusion) | data formatting | bytes 700416 | tf_op jit(solution)/shard_map/gather | solution.py:51
  50.7 3.8 %all-to-all-start = ((bf16[8,171,128]{2,1,0:T(8,128)(2,1)}), bf16[8,171,128]{2,1,0:T(8,128)(2,1)S(1)}, u32[]{:S(2)}, u32[]{:S(2)}) async-start(bf16[8,171,128]{2,1,0:T(8,128)(2,1)} %reshape.291), calls=%async_computation | async-start | bytes 720896 | tf_op jit(solution)/shard_map/all_to_all | solution.py:52
  54.5 0.0 copy-done
  54.5 0.1 copy.10
  54.6 0.1 reshape.300
  54.7 8.7 %all-to-all-done = bf16[8,171,128]{2,1,0:T(8,128)(2,1)S(1)} async-done(((bf16[8,171,128]{2,1,0:T(8,128)(2,1)}), bf16[8,171,128]{2,1,0:T(8,128)(2,1)S(1)}, u32[]{:S(2)}, u32[]{:S(2)}) %all-to-all-start) | async-done | bytes 350240 | tf_op jit(solution)/shard_map/all_to_all | solution.py:52
  63.4 0.1 reshape.288
  63.6 1.9 %gather_fusion.1 = bf16[512,128]{1,0:T(8,128)(2,1)} fusion(bf16[1368,128]{1,0:T(8,128)(2,1)S(1)} %reshape.288, s32[1024]{0:T(1024)S(1)} %pad_clamp_fusion.1), kind=kCustom, calls=%fused_computation.1 | custom fusion | bytes 264192 | tf_op jit(solution)/shard_map/gather | solution.py:54
  65.5 3.3 %all-to-all-start.1 = ((bf16[1,128,4,128]{3,2,0,1:T(4,128)(2,1)}), bf16[1,128,4,128]{3,2,0,1:T(4,128)(2,1)S(1)}, u32[]{:S(2)}, u32[]{:S(2)}) async-start(bf16[1,128,4,128]{3,2,0,1:T(4,128)(2,1)} %bitcast.2), calls=%async_computation.1 | async-start | bytes 262144 | tf_op jit(solution)/shard_map/all_to_all | solution.py:55
  68.8 4.6 %all-to-all-done.1 = bf16[1,128,4,128]{3,2,0,1:T(4,128)(2,1)S(1)} async-done(((bf16[1,128,4,128]{3,2,0,1:T(4,128)(2,1)}), bf16[1,128,4,128]{3,2,0,1:T(4,128)(2,1)S(1)}, u32[]{:S(2)}, u32[]{:S(2)}) %all-to-all-start.1) | async-done | bytes 131104 | tf_op jit(solution)/shard_map/all_to_all | solution.py:55
  73.4 3.4 %convolution_bitcast_fusion = f32[4,32,128]{2,0,1:T(4,128)S(1)} fusion(bf16[32,4,128,128]{3,2,1,0:T(8,128)(2,1)} %param.9, bf16[4,32,4,128]{3,2,1,0:T(4,128)(2,1)S(1)} %bitcast.14), kind=kOutput, calls=%fused_computation.2 | convolution fusion | flops 16777216 | bytes 4390912 | tf_op jit(solution)/shard_map/tkij,ftkj->fti/dot_general | solution.py:56
  76.8 0.1 fusion.1
  76.9 0.1 collective-permute-start.8
  77.0 1.1 %collective-permute-start.9 = (f32[1,32,128]{2,0,1:T(1,128)S(1)}, f32[1,32,128]{2,0,1:T(1,128)S(1)}, u32[]{:S(2)}, u32[]{:S(2)}) collective-permute-start(f32[1,32,128]{2,0,1:T(1,128)S(1)} %get-tuple-element.21), channel_id=1, source_target_pairs={{0,2},{1,3},{2,0},{3,1},{4,6},{5,7},{6,4},{7,5},{8,10},{9,11},{10,... | collective-permute-start | bytes 49160 | tf_op jit(solution)/shard_map/ppermute | solution.py:66
  78.0 0.0 collective-permute-start.10
  78.1 0.3 collective-permute-done.8
  78.4 2.4 %collective-permute-done.9 = f32[1,32,128]{2,0,1:T(1,128)S(1)} collective-permute-done((f32[1,32,128]{2,0,1:T(1,128)S(1)}, f32[1,32,128]{2,0,1:T(1,128)S(1)}, u32[]{:S(2)}, u32[]{:S(2)}) %collective-permute-start.9) | collective-permute-done | bytes 16416 | tf_op jit(solution)/shard_map/ppermute | solution.py:66
  80.8 0.4 collective-permute-done.10
  81.3 0.2 dynamic-slice_reduce_fusion
  81.5 0.6 reshape.289
  (17 shorter events, 0.2 us)
Async XLA Ops:
  1.4 6.2 %collective-permute-start = (f32[1,1,512]{2,1,0:T(1,128)S(1)}, f32[1,1,512]{2,1,0:T(1,128)S(1)}, u32[]{:S(2)}, u32[]{:S(2)}) collective-permute-start(f32[1,1,512]{2,1,0:T(1,128)S(1)} %get-tuple-element.29), channel_id=1, source_target_pairs={{0,4},{4,8},{8,12},{12,16},{16,20},{20,24},{24,28},{1,5},{5,9},{9,... | collective-permute-start | bytes 6152 | tf_op jit(solution)/shard_map/ppermute | solution.py:14
  6.2 5.5 %collective-permute-start.1 = (f32[1,1,512]{2,1,0:T(1,128)S(1)}, f32[1,1,512]{2,1,0:T(1,128)S(1)}, u32[]{:S(2)}, u32[]{:S(2)}) collective-permute-start(f32[1,1,512]{2,1,0:T(1,128)S(1)} %get-tuple-element.30), channel_id=1, source_target_pairs={{4,0},{8,4},{12,8},{16,12},{20,16},{24,20},{28,24},{5,1},{9,5},{13... | collective-permute-start | bytes 6152 | tf_op jit(solution)/shard_map/ppermute | solution.py:17
  12.7 41.8 %copy-start = (s32[128,4]{0,1:T(4,128)S(1)}, s32[128,4]{0,1:T(4,128)}, u32[]{:S(2)}) copy-start(s32[128,4]{0,1:T(4,128)} %param.8) | copy-start | bytes 6148
  13.7 5.7 %collective-permute-start.2 = (f32[1,1,512]{2,1,0:T(1,128)S(1)}, f32[1,1,512]{2,1,0:T(1,128)S(1)}, u32[]{:S(2)}, u32[]{:S(2)}) collective-permute-start(f32[1,1,512]{2,1,0:T(1,128)S(1)} %get-tuple-element.27), channel_id=1, source_target_pairs={{0,4},{4,8},{8,12},{12,16},{16,20},{20,24},{24,28},{1,5},{5,9},{9,... | collective-permute-start | bytes 6152 | tf_op jit(solution)/shard_map/ppermute | solution.py:14
  18.1 5.5 %collective-permute-start.3 = (f32[1,1,512]{2,1,0:T(1,128)S(1)}, f32[1,1,512]{2,1,0:T(1,128)S(1)}, u32[]{:S(2)}, u32[]{:S(2)}) collective-permute-start(f32[1,1,512]{2,1,0:T(1,128)S(1)} %get-tuple-element.28), channel_id=1, source_target_pairs={{4,0},{8,4},{12,8},{16,12},{20,16},{24,20},{28,24},{5,1},{9,5},{13... | collective-permute-start | bytes 6152 | tf_op jit(solution)/shard_map/ppermute | solution.py:17
  24.8 5.5 %collective-permute-start.4 = (f32[1,1,512]{2,1,0:T(1,128)S(1)}, f32[1,1,512]{2,1,0:T(1,128)S(1)}, u32[]{:S(2)}, u32[]{:S(2)}) collective-permute-start(f32[1,1,512]{2,1,0:T(1,128)S(1)} %get-tuple-element.25), channel_id=1, source_target_pairs={{0,4},{4,8},{8,12},{12,16},{16,20},{20,24},{24,28},{1,5},{5,9},{9,... | collective-permute-start | bytes 6152 | tf_op jit(solution)/shard_map/ppermute | solution.py:14
  28.2 5.5 %collective-permute-start.5 = (f32[1,1,512]{2,1,0:T(1,128)S(1)}, f32[1,1,512]{2,1,0:T(1,128)S(1)}, u32[]{:S(2)}, u32[]{:S(2)}) collective-permute-start(f32[1,1,512]{2,1,0:T(1,128)S(1)} %get-tuple-element.26), channel_id=1, source_target_pairs={{4,0},{8,4},{12,8},{16,12},{20,16},{24,20},{28,24},{5,1},{9,5},{13... | collective-permute-start | bytes 6152 | tf_op jit(solution)/shard_map/ppermute | solution.py:17
  34.8 5.7 %collective-permute-start.6 = (f32[1,1,512]{2,1,0:T(1,128)S(1)}, f32[1,1,512]{2,1,0:T(1,128)S(1)}, u32[]{:S(2)}, u32[]{:S(2)}) collective-permute-start(f32[1,1,512]{2,1,0:T(1,128)S(1)} %get-tuple-element.23), channel_id=1, source_target_pairs={{0,4},{4,8},{8,12},{12,16},{16,20},{20,24},{24,28},{1,5},{5,9},{9,... | collective-permute-start | bytes 6152 | tf_op jit(solution)/shard_map/ppermute | solution.py:14
  39.2 5.5 %collective-permute-start.7 = (f32[1,1,512]{2,1,0:T(1,128)S(1)}, f32[1,1,512]{2,1,0:T(1,128)S(1)}, u32[]{:S(2)}, u32[]{:S(2)}) collective-permute-start(f32[1,1,512]{2,1,0:T(1,128)S(1)} %get-tuple-element.24), channel_id=1, source_target_pairs={{4,0},{8,4},{12,8},{16,12},{20,16},{24,20},{28,24},{5,1},{9,5},{13... | collective-permute-start | bytes 6152 | tf_op jit(solution)/shard_map/ppermute | solution.py:17
  50.7 12.7 %all-to-all-start = ((bf16[8,171,128]{2,1,0:T(8,128)(2,1)}), bf16[8,171,128]{2,1,0:T(8,128)(2,1)S(1)}, u32[]{:S(2)}, u32[]{:S(2)}) async-start(bf16[8,171,128]{2,1,0:T(8,128)(2,1)} %reshape.291), calls=%async_computation | async-start | bytes 720896 | tf_op jit(solution)/shard_map/all_to_all | solution.py:52
  65.5 7.9 %all-to-all-start.1 = ((bf16[1,128,4,128]{3,2,0,1:T(4,128)(2,1)}), bf16[1,128,4,128]{3,2,0,1:T(4,128)(2,1)S(1)}, u32[]{:S(2)}, u32[]{:S(2)}) async-start(bf16[1,128,4,128]{3,2,0,1:T(4,128)(2,1)} %bitcast.2), calls=%async_computation.1 | async-start | bytes 262144 | tf_op jit(solution)/shard_map/all_to_all | solution.py:55
  76.9 1.5 %collective-permute-start.8 = (f32[1,32,128]{2,0,1:T(1,128)S(1)}, f32[1,32,128]{2,0,1:T(1,128)S(1)}, u32[]{:S(2)}, u32[]{:S(2)}) collective-permute-start(f32[1,32,128]{2,0,1:T(1,128)S(1)} %get-tuple-element.22), channel_id=1, source_target_pairs={{0,3},{1,0},{2,1},{3,2},{4,7},{5,4},{6,5},{7,6},{8,11},{9,8},{10,9... | collective-permute-start | bytes 49160 | tf_op jit(solution)/shard_map/ppermute | solution.py:66
  77.0 3.8 %collective-permute-start.9 = (f32[1,32,128]{2,0,1:T(1,128)S(1)}, f32[1,32,128]{2,0,1:T(1,128)S(1)}, u32[]{:S(2)}, u32[]{:S(2)}) collective-permute-start(f32[1,32,128]{2,0,1:T(1,128)S(1)} %get-tuple-element.21), channel_id=1, source_target_pairs={{0,2},{1,3},{2,0},{3,1},{4,6},{5,7},{6,4},{7,5},{8,10},{9,11},{10,... | collective-permute-start | bytes 49160 | tf_op jit(solution)/shard_map/ppermute | solution.py:66
  78.0 3.2 %collective-permute-start.10 = (f32[1,32,128]{2,0,1:T(1,128)S(1)}, f32[1,32,128]{2,0,1:T(1,128)S(1)}, u32[]{:S(2)}, u32[]{:S(2)}) collective-permute-start(f32[1,32,128]{2,0,1:T(1,128)S(1)} %get-tuple-element.20), channel_id=1, source_target_pairs={{0,1},{1,2},{2,3},{3,0},{4,5},{5,6},{6,7},{7,4},{8,9},{9,10},{10,1... | collective-permute-start | bytes 49160 | tf_op jit(solution)/shard_map/ppermute | solution.py:66
